TPU v7x, 32 devices: a whole 2x2x4 slice. The times are simulated.
32 devices in a mesh: row: 4 (over y, x), col: 8 (over z, core).
Axes of the slice: x: 2, y: 2, z: 4, core: 2. Of those that a mesh axis runs over, the one named last changes fastest.
Arguments:
- tiles: bfloat16 [256, 256, 256], P(('row', 'col')), may hold values from -0.09375 to 0.09375
- tile_rows: int32 [256], P(('row', 'col')), may hold values from 0 to 3, as said below
- tile_cols: int32 [256], P(('row', 'col')), may hold values from 0 to 1
- tile_count: int32 [32], P(('row', 'col')), may hold values from 0 to 8, as said below
- bounds: float32 [2], replicated, may hold values from -1 to 2, as said below
- vectors: float32 [4096, 128], P(('row', 'col')), may hold values from -6 to 6
Outputs:
- filtered: float32 [4096, 128], P(('row', 'col'))
- gram: float32 [128, 128], replicated
Inputs may be any that keep to these rules, and one draw needn't show every extreme that they name: `tile_rows`: within each device the first tile_count slots name distinct blocks with global block row I <= global block column J; the device's diagonal blocks (I = J) come first; every diagonal block of the Hamiltonian is stored; slots after the live ones hold valid indices but are not part of the matrix. `tile_count`: devices whose block rows all lie below their block columns have no live slot; some device has all 8 slots live. bounds[0] < -0.5 and bounds[1] > 1.0.
All inputs are finite; a program needn't handle non-finite values.
Results may differ from a plain program's by a relative error of at most 0.0037.
Values may be sent and summed in bfloat16 or wider, within the bound.
A program may use at most 64 MiB of HBM per device.

v0:
```python
import jax
import jax.numpy as jnp
from jax import lax
from jax.sharding import PartitionSpec as P

BLK_COL = 2


def spread(block, axis, holder):
    block = jnp.where(lax.axis_index(axis) == holder, block, jnp.zeros_like(block))
    return lax.psum(block, axis)


def on_device(tiles, tile_rows, tile_cols, tile_count, bounds, vectors):
    col_ratio = lax.axis_size("col") // lax.axis_size("row")
    col_index = lax.axis_index("col")
    row_index = lax.axis_index("row")
    root_row = col_index // col_ratio
    slot_total = tiles.shape[0]
    block_size = tiles.shape[1]
    share_rows = vectors.shape[0]
    width_vecs = vectors.shape[1]
    group_rows = share_rows * lax.axis_size("col")
    group_blocks = group_rows // block_size
    column_rows = BLK_COL * block_size
    total_rows = share_rows * lax.axis_size("row") * lax.axis_size("col")
    offset = col_index % col_ratio * column_rows
    live_mask = (jnp.arange(slot_total, dtype=jnp.int32) < tile_count[0]).astype(jnp.bfloat16)
    owner_flag = (row_index == root_row).astype(jnp.float32)
    center = (bounds[1] + bounds[0]) * 0.5
    halfwidth = (bounds[1] - bounds[0]) * 0.5

    def apply_hamiltonian(current_vec):
        vector_panel = current_vec.astype(jnp.bfloat16)
        row_panel = lax.all_gather(vector_panel, "col", axis=0, tiled=True)
        col_piece = lax.dynamic_slice_in_dim(row_panel, offset, column_rows, 0)
        col_panel = spread(col_piece, "row", root_row)
        row_input = row_panel.reshape(group_blocks, block_size, width_vecs)
        col_input = col_panel.reshape(BLK_COL, block_size, width_vecs)
        start_rows = jnp.zeros((group_blocks, block_size, width_vecs), jnp.float32)
        start_cols = jnp.zeros((BLK_COL, block_size, width_vecs), jnp.float32)
        masked_cols = col_input[tile_cols] * live_mask[:, None, None]
        masked_rows = row_input[tile_rows] * live_mask[:, None, None]
        forward = jnp.einsum("tab,tbk->tak", tiles, masked_cols, preferred_element_type=jnp.float32)
        backward = jnp.einsum(
            "tab,tak->tbk", tiles, masked_rows, preferred_element_type=jnp.float32
        )
        row_part = start_rows.at[tile_rows].add(forward)
        col_part = start_cols.at[tile_cols].add(backward)
        column_total = lax.psum(col_part, "row")
        row_part = row_part.reshape(group_rows, width_vecs)
        present = lax.dynamic_slice_in_dim(row_part, offset, column_rows, 0)
        updated = present + owner_flag * column_total.reshape(column_rows, width_vecs)
        row_part = lax.dynamic_update_slice_in_dim(row_part, updated, offset, 0)
        return lax.psum_scatter(row_part, "col", scatter_dimension=0, tiled=True)

    current_vec = (apply_hamiltonian(vectors) - center * vectors) / halfwidth
    image = apply_hamiltonian(current_vec)
    following = 2.0 * (image - center * current_vec) / halfwidth - vectors
    current_vec = following
    gram_local = lax.dot_general(
        current_vec,
        current_vec,
        (((0,), (0,)), ((), ())),
        precision=lax.Precision.HIGHEST,
        preferred_element_type=jnp.float32,
    )
    gram_total = lax.psum(gram_local, ("row", "col"))
    return (current_vec, gram_total / total_rows)


def solution(mesh):
    in_specs = (
        P(("row", "col"), None, None),
        P(("row", "col")),
        P(("row", "col")),
        P(("row", "col")),
        P(),
        P(("row", "col"), None),
    )
    out_specs = (P(("row", "col"), None), P())
    return jax.shard_map(
        on_device, mesh=mesh, in_specs=in_specs, out_specs=out_specs, check_vma=False
    )
```

profile of v0, /device:TPU:1, one launch (start us, length us, event | category | flops | bytes accessed | tf_op | source)
XLA Modules:
  0.0 414.4 jit_solution(1064199134010569408)
XLA Ops:
  7.2 0.0 copy-start
  7.2 0.0 all-reduce.6.cloned.1.call-start
  7.2 0.9 convert_element_type.16
  8.2 15.8 %all_gather.6 = bf16[1024,128]{1,0:T(8,128)(2,1)S(1)} all-gather(bf16[128,128]{1,0:T(8,128)(2,1)S(1)} %convert_element_type.16), channel_id=1, replica_groups=mesh['row'=4,'col'=8] {'col'}, dimensions={0}, use_global_device_ids=true | all-gather | bytes 294912 | tf_op jit(solution)/shard_map/all_gather | solution.py:35
  23.9 0.7 dynamic-slice_select_fusion.1
  24.6 0.0 all-reduce.6.cloned.1.call-update
  24.6 0.0 all-reduce.8.cloned.1.call-start
  25.3 0.0 copy-start.9
  25.4 0.6 copy-done.9
  26.0 0.6 gather_fusion.1
  26.7 0.4 convolution_bitcast_fusion.2
  27.1 0.0 copy-start.10
  27.1 0.3 copy.15
  27.4 0.3 copy-done.10
  27.8 1.3 scatter_fusion.1
  29.1 0.0 copy-start.4
  29.1 0.7 copy-done.4
  29.8 0.0 all-reduce.8.cloned.1.call-update
  29.8 0.0 reduce-scatter.3.cloned.1.call-start
  29.9 37.0 %all-reduce.6.cloned.1.call-done = bf16[2,256,128]{2,1,0:T(8,128)(2,1)} async-done(((bf16[2,256,128]{2,1,0:T(8,128)(2,1)}), bf16[2,256,128]{2,1,0:T(8,128)(2,1)}) %all-reduce.6.cloned.1.call-update) | async-done | bytes 131088 | tf_op jit(solution)/shard_map/psum | solution.py:11
  66.9 1.5 gather_fusion
  68.5 1.7 convolution_bitcast_fusion.3
  70.2 1.5 copy.13
  71.8 1.3 scatter_fusion
  73.1 39.9 %all-reduce.8.cloned.1.call-done = f32[2,256,128]{2,1,0:T(8,128)} async-done(((f32[2,256,128]{2,1,0:T(8,128)}), f32[2,256,128]{2,1,0:T(8,128)}) %all-reduce.8.cloned.1.call-update) | async-done | bytes 262160 | tf_op jit(solution)/shard_map/psum | solution.py:50
  113.1 1.0 broadcast_multiply_fusion.1
  114.0 0.1 constant_dynamic-update-slice_fusion.1
  114.1 0.0 copy-start.8
  114.1 0.0 copy-start.5
  114.1 0.8 copy-done.2
  114.9 0.0 reduce-scatter.3.cloned.1.call-update
  114.9 0.0 all-reduce.10.cloned.1.call-start
  114.9 0.6 fusion.9
  118.1 25.2 %reduce-scatter.3.cloned.1.call-done = f32[128,128]{1,0:T(8,128)} async-done(((f32[1024,128]{1,0:T(8,128)}), f32[128,128]{1,0:T(8,128)}) %reduce-scatter.3.cloned.1.call-update) | async-done | bytes 65552 | tf_op jit(solution)/shard_map/reduce_scatter | solution.py:55
  143.4 0.9 fusion.8
  144.2 18.0 %all_gather.7 = bf16[1024,128]{1,0:T(8,128)(2,1)S(1)} all-gather(bf16[128,128]{1,0:T(8,128)(2,1)S(1)} %fusion.8), channel_id=1, replica_groups=mesh['row'=4,'col'=8] {'col'}, dimensions={0}, use_global_device_ids=true | all-gather | bytes 294912 | tf_op jit(solution)/shard_map/all_gather | solution.py:35
  162.3 0.7 dynamic-slice_select_fusion
  162.9 0.6 gather_fusion.3
  163.6 0.0 all-reduce.10.cloned.1.call-update
  163.6 0.0 all-reduce.12.cloned.1.call-start
  163.7 0.4 convolution_bitcast_fusion
  164.1 0.3 copy.19
  164.4 1.3 scatter_fusion.3
  165.8 0.7 copy-done.3
  166.5 0.0 all-reduce.12.cloned.1.call-update
  166.5 0.0 reduce-scatter.5.cloned.1.call-start
  166.6 36.5 %all-reduce.10.cloned.1.call-done = bf16[2,256,128]{2,1,0:T(8,128)(2,1)} async-done(((bf16[2,256,128]{2,1,0:T(8,128)(2,1)}), bf16[2,256,128]{2,1,0:T(8,128)(2,1)}) %all-reduce.10.cloned.1.call-update) | async-done | bytes 131088 | tf_op jit(solution)/shard_map/psum | solution.py:11
  203.1 1.5 gather_fusion.2
  204.7 1.7 convolution_bitcast_fusion.1
  206.4 1.5 copy.17
  208.0 1.3 scatter_fusion.2
  209.3 39.5 %all-reduce.12.cloned.1.call-done = f32[2,256,128]{2,1,0:T(8,128)} async-done(((f32[2,256,128]{2,1,0:T(8,128)}), f32[2,256,128]{2,1,0:T(8,128)}) %all-reduce.12.cloned.1.call-update) | async-done | bytes 262160 | tf_op jit(solution)/shard_map/psum | solution.py:50
  248.8 1.0 broadcast_multiply_fusion
  249.8 0.1 constant_dynamic-update-slice_fusion
  249.9 0.8 copy-done.1
  250.7 0.0 reduce-scatter.5.cloned.1.call-update
  250.7 0.0 all-reduce.14.cloned.1.call-start
  250.7 28.2 %reduce-scatter.5.cloned.1.call-done = f32[128,128]{1,0:T(8,128)} async-done(((f32[1024,128]{1,0:T(8,128)}), f32[128,128]{1,0:T(8,128)}) %reduce-scatter.5.cloned.1.call-update) | async-done | bytes 65552 | tf_op jit(solution)/shard_map/reduce_scatter | solution.py:55
  278.9 0.9 divide_subtract_fusion
  279.8 0.0 copy-start.6
  279.8 0.9 fusion.10
  280.7 0.0 all-reduce.14.cloned.1.call-update
  280.8 125.3 %all-reduce.14.cloned.1.call-done = f32[128,128]{1,0:T(8,128)} async-done(((f32[128,128]{1,0:T(8,128)}), f32[128,128]{1,0:T(8,128)}) %all-reduce.14.cloned.1.call-update) | async-done | bytes 65552 | tf_op jit(solution)/shard_map/psum | solution.py:68
  406.1 1.5 broadcast_multiply_fusion.2
  (18 shorter events, 0.2 us)
Async XLA Ops:
  7.2 19.5 %copy-start = (bf16[8,256,256]{2,1,0:T(8,128)(2,1)S(1)}, bf16[8,256,256]{2,1,0:T(8,128)(2,1)}, u32[]{:S(2)}) copy-start(bf16[8,256,256]{2,1,0:T(8,128)(2,1)} %param.6) | copy-start | bytes 3145732
  7.2 59.8 %all-reduce.6.cloned.1.call-start = ((), (), s32[]{:S(2)}) async-start(), calls=%async_computation.2 | async-start | bytes 262144 | tf_op jit(solution)/shard_map/psum | solution.py:11
  24.6 88.4 %all-reduce.8.cloned.1.call-start = ((), (), s32[]{:S(2)}) async-start(), calls=%async_computation.3 | async-start | bytes 524288 | tf_op jit(solution)/shard_map/psum | solution.py:50
  25.3 0.7 copy-start.9
  27.1 0.7 copy-start.10
  29.1 0.7 copy-start.4
  29.8 113.5 %reduce-scatter.3.cloned.1.call-start = ((), (), s32[]{:S(2)}) async-start(), calls=%async_computation.4 | async-start | bytes 589824 | tf_op jit(solution)/shard_map/reduce_scatter | solution.py:55
  114.1 0.8 copy-start.2
  114.1 0.9 copy-start.8
  114.1 29.3 %copy-start.5 = (f32[128,128]{1,0:T(8,128)S(1)}, f32[128,128]{1,0:T(8,128)}, u32[]{:S(2)}) copy-start(f32[128,128]{1,0:T(8,128)} %param.11) | copy-start | bytes 196612
  114.9 88.2 %all-reduce.10.cloned.1.call-start = ((), (), s32[]{:S(2)}) async-start(), calls=%async_computation.5 | async-start | bytes 262144 | tf_op jit(solution)/shard_map/psum | solution.py:11
  163.6 85.2 %all-reduce.12.cloned.1.call-start = ((), (), s32[]{:S(2)}) async-start(), calls=%async_computation.6 | async-start | bytes 524288 | tf_op jit(solution)/shard_map/psum | solution.py:50
  165.8 0.7 copy-start.3
  166.5 112.4 %reduce-scatter.5.cloned.1.call-start = ((), (), s32[]{:S(2)}) async-start(), calls=%async_computation.7 | async-start | bytes 589824 | tf_op jit(solution)/shard_map/reduce_scatter | solution.py:55
  249.9 0.8 copy-start.1
  249.9 29.1 %copy-start.7 = (f32[128,128]{1,0:T(8,128)S(1)}, f32[128,128]{1,0:T(8,128)}, u32[]{:S(2)}) copy-start(f32[128,128]{1,0:T(8,128)} %reduce-scatter.3.cloned.1.call-done) | copy-start | bytes 196612
  250.7 155.4 %all-reduce.14.cloned.1.call-start = ((), (), s32[]{:S(2)}) async-start(), calls=%async_computation.8 | async-start | bytes 131072 | tf_op jit(solution)/shard_map/psum | solution.py:68
  279.8 0.9 copy-start.6
Sparse Core Ops, SparseCore 0:
  24.8 42.1 all-reduce.5
  70.1 42.8 all-reduce.7
  115.3 28.0 reduce-scatter.2
  163.7 39.3 all-reduce.9
  205.9 42.9 all-reduce.11
  251.0 27.8 reduce-scatter.4
  285.1 120.9 all-reduce.13
where the time goes:
time: 415 us; the launch traced here: 414 us
  waiting for transfers between devices  332 us (80%)
  blocking collectives  33.8 us (8%)
  between operations  17.7 us (4%)
  local copies, waits for them, and re-layouts  12.8 us (3%)
  other arithmetic  12.8 us (3%)
  matrix products  5.15 us (1%)
    psum x1, waiting for transfers between devices, on_device(): gram_total = lax.psum(gram_local, ('row', 'col'))  125 us
    psum x2, waiting for transfers between devices, apply_hamiltonian(): column_total = lax.psum(col_part, 'row')  79.5 us
    psum x2, waiting for transfers between devices, spread(): return lax.psum(block, axis)  73.6 us
    reduce_scatter x2, waiting for transfers between devices, apply_hamiltonian(): return lax.psum_scatter(row_part, 'col', scatter_dimension=0, tiled=True)  53.5 us
    all_gather x2, blocking collectives, apply_hamiltonian(): row_panel = lax.all_gather(vector_panel, 'col', axis=0, tiled=True)  33.8 us
  transfers between devices with their start and end apart: 7, of which 7 were waited for; matrix products, arithmetic and copies ran while one was open for 4% of the time, Pallas kernels for 0%

commit v1 on v0

--- a/solution.py
+++ b/solution.py
@@ -2,6 +2,7 @@
 import jax.numpy as jnp
 from jax import lax
 from jax.sharding import PartitionSpec as P
+from jax.lax import psum
 
 BLK_COL = 2
 
@@ -65,7 +66,15 @@
         precision=lax.Precision.HIGHEST,
         preferred_element_type=jnp.float32,
     )
-    gram_total = lax.psum(gram_local, ("row", "col"))
+
+    def replace_quarters(mat):
+        net_axis = "row"
+        shard_axis = "col"
+        for pp in (shard_axis, net_axis):
+            mat = psum(mat, pp)
+        return mat
+
+    gram_total = replace_quarters(gram_local)
     return (current_vec, gram_total / total_rows)
 
 

time: 415 us -> 390 us (0.940)
  waiting for transfers between devices: 332 us -> 306 us
    psum x1 -> x2, waiting for transfers between devices: 125 us -> 99.6 us  [replace_quarters(): mat = psum(mat, pp)]
  transfers between devices with their start and end apart: 7 -> 8, of which waited for: 7 -> 8; matrix products, arithmetic and copies ran while one was open for 4% -> 5% of each run, Pallas kernels for 0% -> 0%
where the time goes in v1:
time: 390 us; the launch traced here: 389 us
  waiting for transfers between devices  306 us (78%)
  blocking collectives  33.8 us (9%)
  between operations  17.7 us (5%)
  local copies, waits for them, and re-layouts  12.8 us (3%)
  other arithmetic  12.8 us (3%)
  matrix products  5.15 us (1%)
    psum x2, waiting for transfers between devices, replace_quarters(): mat = psum(mat, pp)  99.6 us
    psum x2, waiting for transfers between devices, apply_hamiltonian(): column_total = lax.psum(col_part, 'row')  79.5 us
    psum x2, waiting for transfers between devices, spread(): return lax.psum(block, axis)  73.6 us
    reduce_scatter x2, waiting for transfers between devices, apply_hamiltonian(): return lax.psum_scatter(row_part, 'col', scatter_dimension=0, tiled=True)  53.5 us
    all_gather x2, blocking collectives, apply_hamiltonian(): row_panel = lax.all_gather(vector_panel, 'col', axis=0, tiled=True)  33.8 us
  transfers between devices with their start and end apart: 8, of which 8 were waited for; matrix products, arithmetic and copies ran while one was open for 5% of the time, Pallas kernels for 0%

profile of v1, /device:TPU:1, one launch (start us, length us, event | category | flops | bytes accessed | tf_op | source)
XLA Modules:
  0.0 388.7 jit_solution(13589876530114365089)
XLA Ops:
  7.2 0.0 copy-start
  7.2 0.0 all-reduce.7.cloned.1.call-start
  7.2 0.9 convert_element_type.16
  8.2 15.8 %all_gather.6 = bf16[1024,128]{1,0:T(8,128)(2,1)S(1)} all-gather(bf16[128,128]{1,0:T(8,128)(2,1)S(1)} %convert_element_type.16), channel_id=1, replica_groups=mesh['row'=4,'col'=8] {'col'}, dimensions={0}, use_global_device_ids=true | all-gather | bytes 294912 | tf_op jit(solution)/shard_map/all_gather | solution.py:36
  23.9 0.7 dynamic-slice_select_fusion.1
  24.6 0.0 all-reduce.7.cloned.1.call-update
  24.6 0.0 all-reduce.9.cloned.1.call-start
  25.3 0.0 copy-start.9
  25.4 0.6 copy-done.9
  26.0 0.6 gather_fusion.1
  26.7 0.4 convolution_bitcast_fusion.2
  27.1 0.0 copy-start.10
  27.1 0.3 copy.15
  27.4 0.3 copy-done.10
  27.8 1.3 scatter_fusion.1
  29.1 0.7 copy-done.4
  29.8 0.0 all-reduce.9.cloned.1.call-update
  29.8 0.0 reduce-scatter.3.cloned.1.call-start
  29.9 37.0 %all-reduce.7.cloned.1.call-done = bf16[2,256,128]{2,1,0:T(8,128)(2,1)} async-done(((bf16[2,256,128]{2,1,0:T(8,128)(2,1)}), bf16[2,256,128]{2,1,0:T(8,128)(2,1)}) %all-reduce.7.cloned.1.call-update) | async-done | bytes 131088 | tf_op jit(solution)/shard_map/psum | solution.py:12
  66.9 1.5 gather_fusion
  68.5 1.7 convolution_bitcast_fusion.3
  70.2 1.5 copy.13
  71.8 1.3 scatter_fusion
  73.1 39.9 %all-reduce.9.cloned.1.call-done = f32[2,256,128]{2,1,0:T(8,128)} async-done(((f32[2,256,128]{2,1,0:T(8,128)}), f32[2,256,128]{2,1,0:T(8,128)}) %all-reduce.9.cloned.1.call-update) | async-done | bytes 262160 | tf_op jit(solution)/shard_map/psum | solution.py:51
  113.1 1.0 broadcast_multiply_fusion.1
  114.0 0.1 constant_dynamic-update-slice_fusion.1
  114.1 0.8 copy-done.2
  114.9 0.0 reduce-scatter.3.cloned.1.call-update
  114.9 0.0 all-reduce.11.cloned.1.call-start
  114.9 0.6 fusion.9
  118.1 25.2 %reduce-scatter.3.cloned.1.call-done = f32[128,128]{1,0:T(8,128)} async-done(((f32[1024,128]{1,0:T(8,128)}), f32[128,128]{1,0:T(8,128)}) %reduce-scatter.3.cloned.1.call-update) | async-done | bytes 65552 | tf_op jit(solution)/shard_map/reduce_scatter | solution.py:56
  143.4 0.9 fusion.8
  144.2 18.0 %all_gather.7 = bf16[1024,128]{1,0:T(8,128)(2,1)S(1)} all-gather(bf16[128,128]{1,0:T(8,128)(2,1)S(1)} %fusion.8), channel_id=1, replica_groups=mesh['row'=4,'col'=8] {'col'}, dimensions={0}, use_global_device_ids=true | all-gather | bytes 294912 | tf_op jit(solution)/shard_map/all_gather | solution.py:36
  162.3 0.7 dynamic-slice_select_fusion
  162.9 0.6 gather_fusion.3
  163.6 0.0 all-reduce.11.cloned.1.call-update
  163.6 0.0 all-reduce.13.cloned.1.call-start
  163.7 0.4 convolution_bitcast_fusion
  164.1 0.3 copy.19
  164.4 1.3 scatter_fusion.3
  165.8 0.7 copy-done.3
  166.5 0.0 all-reduce.13.cloned.1.call-update
  166.5 0.0 reduce-scatter.5.cloned.1.call-start
  166.6 36.5 %all-reduce.11.cloned.1.call-done = bf16[2,256,128]{2,1,0:T(8,128)(2,1)} async-done(((bf16[2,256,128]{2,1,0:T(8,128)(2,1)}), bf16[2,256,128]{2,1,0:T(8,128)(2,1)}) %all-reduce.11.cloned.1.call-update) | async-done | bytes 131088 | tf_op jit(solution)/shard_map/psum | solution.py:12
  203.1 1.5 gather_fusion.2
  204.7 1.7 convolution_bitcast_fusion.1
  206.4 1.5 copy.17
  208.0 1.3 scatter_fusion.2
  209.3 39.5 %all-reduce.13.cloned.1.call-done = f32[2,256,128]{2,1,0:T(8,128)} async-done(((f32[2,256,128]{2,1,0:T(8,128)}), f32[2,256,128]{2,1,0:T(8,128)}) %all-reduce.13.cloned.1.call-update) | async-done | bytes 262160 | tf_op jit(solution)/shard_map/psum | solution.py:51
  248.8 1.0 broadcast_multiply_fusion
  249.8 0.1 constant_dynamic-update-slice_fusion
  249.9 0.8 copy-done.1
  250.7 0.0 reduce-scatter.5.cloned.1.call-update
  250.7 0.0 all-reduce.15.cloned.1.call-start
  250.7 28.2 %reduce-scatter.5.cloned.1.call-done = f32[128,128]{1,0:T(8,128)} async-done(((f32[1024,128]{1,0:T(8,128)}), f32[128,128]{1,0:T(8,128)}) %reduce-scatter.5.cloned.1.call-update) | async-done | bytes 65552 | tf_op jit(solution)/shard_map/reduce_scatter | solution.py:56
  278.9 0.9 divide_subtract_fusion
  279.8 0.0 copy-start.6
  279.8 0.9 fusion.10
  280.7 0.0 all-reduce.15.cloned.1.call-update
  280.8 0.0 all-reduce.17.cloned.1.call-start
  280.8 54.7 %all-reduce.15.cloned.1.call-done = f32[128,128]{1,0:T(8,128)} async-done(((f32[128,128]{1,0:T(8,128)}), f32[128,128]{1,0:T(8,128)}) %all-reduce.15.cloned.1.call-update) | async-done | bytes 65552 | tf_op jit(solution)/shard_map/psum | solution.py:74
  335.6 0.0 all-reduce.17.cloned.1.call-update
  335.6 44.8 %all-reduce.17.cloned.1.call-done = f32[128,128]{1,0:T(8,128)} async-done(((f32[128,128]{1,0:T(8,128)}), f32[128,128]{1,0:T(8,128)}) %all-reduce.17.cloned.1.call-update) | async-done | bytes 65552 | tf_op jit(solution)/shard_map/psum | solution.py:74
  380.4 1.5 broadcast_multiply_fusion.2
  (21 shorter events, 0.2 us)
Async XLA Ops:
  7.2 19.5 %copy-start = (bf16[8,256,256]{2,1,0:T(8,128)(2,1)S(1)}, bf16[8,256,256]{2,1,0:T(8,128)(2,1)}, u32[]{:S(2)}) copy-start(bf16[8,256,256]{2,1,0:T(8,128)(2,1)} %param.6) | copy-start | bytes 3145732
  7.2 59.8 %all-reduce.7.cloned.1.call-start = ((), (), s32[]{:S(2)}) async-start(), calls=%async_computation.2 | async-start | bytes 262144 | tf_op jit(solution)/shard_map/psum | solution.py:12
  24.6 88.4 %all-reduce.9.cloned.1.call-start = ((), (), s32[]{:S(2)}) async-start(), calls=%async_computation.3 | async-start | bytes 524288 | tf_op jit(solution)/shard_map/psum | solution.py:51
  25.3 0.7 copy-start.9
  27.1 0.7 copy-start.10
  29.1 0.7 copy-start.4
  29.8 113.5 %reduce-scatter.3.cloned.1.call-start = ((), (), s32[]{:S(2)}) async-start(), calls=%async_computation.4 | async-start | bytes 589824 | tf_op jit(solution)/shard_map/reduce_scatter | solution.py:56
  114.1 0.8 copy-start.2
  114.1 0.9 copy-start.8
  114.1 29.3 %copy-start.5 = (f32[128,128]{1,0:T(8,128)S(1)}, f32[128,128]{1,0:T(8,128)}, u32[]{:S(2)}) copy-start(f32[128,128]{1,0:T(8,128)} %param.11) | copy-start | bytes 196612
  114.9 88.2 %all-reduce.11.cloned.1.call-start = ((), (), s32[]{:S(2)}) async-start(), calls=%async_computation.5 | async-start | bytes 262144 | tf_op jit(solution)/shard_map/psum | solution.py:12
  163.6 85.2 %all-reduce.13.cloned.1.call-start = ((), (), s32[]{:S(2)}) async-start(), calls=%async_computation.6 | async-start | bytes 524288 | tf_op jit(solution)/shard_map/psum | solution.py:51
  165.8 0.7 copy-start.3
  166.5 112.4 %reduce-scatter.5.cloned.1.call-start = ((), (), s32[]{:S(2)}) async-start(), calls=%async_computation.7 | async-start | bytes 589824 | tf_op jit(solution)/shard_map/reduce_scatter | solution.py:56
  249.9 0.8 copy-start.1
  249.9 29.1 %copy-start.7 = (f32[128,128]{1,0:T(8,128)S(1)}, f32[128,128]{1,0:T(8,128)}, u32[]{:S(2)}) copy-start(f32[128,128]{1,0:T(8,128)} %reduce-scatter.3.cloned.1.call-done) | copy-start | bytes 196612
  250.7 84.9 %all-reduce.15.cloned.1.call-start = ((), (), s32[]{:S(2)}) async-start(), calls=%async_computation.8 | async-start | bytes 131072 | tf_op jit(solution)/shard_map/psum | solution.py:74
  279.8 0.9 copy-start.6
  280.8 99.6 %all-reduce.17.cloned.1.call-start = ((), (), s32[]{:S(2)}) async-start(), calls=%async_computation.9 | async-start | bytes 131072 | tf_op jit(solution)/shard_map/psum | solution.py:74
Sparse Core Ops, SparseCore 0:
  24.8 42.1 all-reduce.6
  70.1 42.8 all-reduce.8
  115.3 28.0 reduce-scatter.2
  163.7 39.3 all-reduce.10
  205.9 42.9 all-reduce.12
  251.0 27.8 reduce-scatter.4
  281.8 53.6 all-reduce.14
  338.7 41.6 all-reduce.16
